TPU v7x, 512 devices: a whole 4x4x16 slice. The times are simulated.
512 devices in a mesh: row: 16 (over z), col: 32 (over y, x, core).
Axes of the slice: x: 4, y: 4, z: 16, core: 2. Of those that a mesh axis runs over, the one named last changes fastest.
Arguments:
- tokens: bfloat16 [2048, 8192], P('col', 'row'), may hold values from -6 to 6
- cotangent: bfloat16 [2048, 8192], P('col', 'row'), may hold values from -42.33202 to 42.33202
- gate_pre: bfloat16 [2048, 14336], P('row', 'col'), may hold values from -6 to 6
- up_act: bfloat16 [2048, 14336], P('row', 'col'), may hold values from -6 to 6
- gate_weight: bfloat16 [8192, 14336], P('row', 'col'), may hold values from -6 to 6
- up_weight: bfloat16 [8192, 14336], P('row', 'col'), may hold values from -6 to 6
- down_weight: bfloat16 [14336, 8192], P('col', 'row'), may hold values from -9 to 9
- moment_m: bfloat16 [14336, 8192], P('col', 'row'), may hold values from -6 to 6
- moment_v: bfloat16 [14336, 8192], P('col', 'row'), may hold values from 0.1 to 1.6015625
Outputs:
- grad_input: bfloat16 [2048, 8192], P('col', 'row')
- grad_gate: bfloat16 [8192, 14336], P('row', 'col')
- grad_up: bfloat16 [8192, 14336], P('row', 'col')
- new_m: bfloat16 [14336, 8192], P('col', 'row')
- new_v: bfloat16 [14336, 8192], P('col', 'row')
- step_down: bfloat16 [14336, 8192], P('col', 'row')
- trust_ratio: float32 [], replicated
All inputs are finite; a program needn't handle non-finite values.
Results may differ from a plain program's by a relative error of at most 0.03.
Values may be sent and summed in bfloat16 or wider, within the bound.
No kernel may reach another device: no remote copies, remote signals or barrier semaphores. Data moves between devices by JAX's collectives and lax.ppermute only.
A program may use at most 64 MiB of HBM per device.

v0:
```python
import jax
import jax.numpy as jnp
from jax import lax
from jax.sharding import PartitionSpec as P

D = 8192
FF = 14336


def activation_grads(grad_hidden, gate_pre, up_act):
    gate_vals = gate_pre.astype(jnp.float32)
    up_vals = up_act.astype(jnp.float32)
    sigma = jax.nn.sigmoid(gate_vals)
    swish = gate_vals * sigma
    hidden = (swish * up_vals).astype(jnp.bfloat16)
    grad_upact = (grad_hidden * swish).astype(jnp.bfloat16)
    grad_gateact = (grad_hidden * up_vals * sigma * (1.0 + gate_vals * (1.0 - sigma))).astype(
        jnp.bfloat16
    )
    return (hidden, grad_gateact, grad_upact)


def shards(
    tokens, cotangent, gate_pre, up_act, gate_weight, up_weight, down_weight, moment_m, moment_v
):
    scale_width = float(D) ** (-0.5)
    scale_hidden = float(FF) ** (-0.5)
    contract_last = (((1,), (1,)), ((), ()))
    contract_first = (((0,), (0,)), ((), ()))
    weight_vals = down_weight.astype(jnp.float32)
    tokens_all, cotangent_all = (
        lax.all_gather(tokens, "col", axis=0, tiled=True),
        lax.all_gather(cotangent, "col", axis=0, tiled=True),
    )
    grad_hidden = lax.psum_scatter(
        (
            lax.dot_general(
                cotangent_all, down_weight, contract_last, preferred_element_type=jnp.float32
            )
            * scale_hidden
        ).astype(jnp.bfloat16),
        "row",
        scatter_dimension=0,
        tiled=True,
    ).astype(jnp.float32)
    hidden, grad_gateact, grad_upact = activation_grads(grad_hidden, gate_pre, up_act)
    hidden_all, gateact_all, upact_all = (
        lax.all_gather(hidden, "row", axis=0, tiled=True),
        lax.all_gather(grad_gateact, "row", axis=0, tiled=True),
        lax.all_gather(grad_upact, "row", axis=0, tiled=True),
    )
    grad_down = (
        lax.dot_general(
            hidden_all, cotangent_all, contract_first, preferred_element_type=jnp.float32
        )
        * scale_hidden
    )
    grad_gate = (
        lax.dot_general(tokens_all, gateact_all, contract_first, preferred_element_type=jnp.float32)
        * scale_width
    ).astype(jnp.bfloat16)
    grad_up = (
        lax.dot_general(tokens_all, upact_all, contract_first, preferred_element_type=jnp.float32)
        * scale_width
    ).astype(jnp.bfloat16)
    total = lax.dot_general(
        gateact_all, gate_weight, contract_last, preferred_element_type=jnp.float32
    )
    total = total + lax.dot_general(
        upact_all, up_weight, contract_last, preferred_element_type=jnp.float32
    )
    grad_input = lax.psum_scatter(
        (total * scale_width).astype(jnp.bfloat16), "col", scatter_dimension=0, tiled=True
    )
    first = 0.9 * moment_m.astype(jnp.float32) + 0.1 * grad_down
    second = 0.95 * moment_v.astype(jnp.float32) + 0.05 * grad_down * grad_down
    update = first / (jnp.sqrt(second) + 1e-08) + 0.1 * weight_vals
    update_local = jnp.sum(update * update)
    weight_total, update_total = lax.psum(
        (jnp.sum(weight_vals * weight_vals), update_local), ("row", "col")
    )
    trust_ratio = jnp.sqrt(weight_total) / jnp.sqrt(update_total + 1e-06)
    step_down = (trust_ratio * update).astype(jnp.bfloat16)
    return (
        grad_input,
        grad_gate,
        grad_up,
        first.astype(jnp.bfloat16),
        second.astype(jnp.bfloat16),
        step_down,
        trust_ratio,
    )


def solution(mesh):
    in_specs = (
        P("col", "row"),
        P("col", "row"),
        P("row", "col"),
        P("row", "col"),
        P("row", "col"),
        P("row", "col"),
        P("col", "row"),
        P("col", "row"),
        P("col", "row"),
    )
    out_specs = (
        P("col", "row"),
        P("row", "col"),
        P("row", "col"),
        P("col", "row"),
        P("col", "row"),
        P("col", "row"),
        P(),
    )
    return jax.shard_map(shards, mesh=mesh, in_specs=in_specs, out_specs=out_specs, check_vma=False)
```

profile of v0, /device:TPU:1, one launch (start us, length us, event | category | flops | bytes accessed | tf_op | source)
XLA Modules:
  0.0 553.5 jit_solution(14277267728744299186)
XLA Ops:
  7.2 0.0 copy-start
  7.2 0.0 all-gather.6.cloned.1.call-start
  7.2 0.7 all-gather.6.cloned.1.call-update
  7.9 0.0 reduce-scatter.7.cloned.1.call-start
  8.0 68.1 %all-gather.6.cloned.1.call-done = bf16[2048,512]{1,0:T(8,128)(2,1)} async-done(((bf16[64,512]{1,0:T(8,128)(2,1)}), bf16[2048,512]{1,0:T(8,128)(2,1)}) %all-gather.6.cloned.1.call-update) | async-done | bytes 2097168 | tf_op jit(solution)/shard_map/all_gather | solution.py:33
  76.1 2.8 multiply_convert_fusion.1
  78.9 2.5 copy.16
  81.3 0.0 copy-start.3
  81.3 0.0 copy-start.4
  81.3 0.0 reduce-scatter.7.cloned.1.call-update
  81.4 0.0 all-gather.8.cloned.1.call-start
  81.4 62.2 %reduce-scatter.7.cloned.1.call-done = bf16[128,448]{1,0:T(8,128)(2,1)} async-done(((bf16[2048,448]{1,0:T(8,128)(2,1)}), bf16[128,448]{1,0:T(8,128)(2,1)}) %reduce-scatter.7.cloned.1.call-update) | async-done | bytes 114704
  143.6 1.0 copy.17
  144.6 0.0 copy-done.3
  144.6 0.0 copy-done.4
  144.6 0.8 fusion.12
  145.5 0.0 all-gather.8.cloned.1.call-update
  145.5 0.0 all-gather.10.cloned.1.call-start
  145.6 0.5 all-gather.10.cloned.1.call-update
  146.1 0.0 all-gather.14.cloned.1.call-start
  146.1 0.5 all-gather.14.cloned.1.call-update
  146.7 0.0 all-gather.12.cloned.1.call-start
  146.7 0.5 all-gather.12.cloned.1.call-update
  147.3 0.0 copy-start.2
  147.3 0.0 reduce-scatter.5.cloned.1.call-start
  147.3 73.1 %all-gather.8.cloned.1.call-done = bf16[2048,448]{0,1:T(8,128)(2,1)} async-done(((bf16[128,448]{0,1:T(8,128)(2,1)}), bf16[2048,448]{0,1:T(8,128)(2,1)}) %all-gather.8.cloned.1.call-update) | async-done | bytes 1835024 | tf_op jit(solution)/shard_map/all_gather | solution.py:49
  220.4 0.0 copy-done
  220.4 4.8 fusion.18
  225.2 70.8 %all-gather.10.cloned.1.call-done = bf16[2048,448]{0,1:T(8,128)(2,1)} async-done(((bf16[128,448]{0,1:T(8,128)(2,1)}), bf16[2048,448]{0,1:T(8,128)(2,1)}) %all-gather.10.cloned.1.call-update) | async-done | bytes 1835024 | tf_op jit(solution)/shard_map/all_gather | solution.py:50
  295.9 0.0 copy-done.2
  295.9 5.4 multiply_convert_fusion
  301.3 0.0 copy-start.5
  301.3 0.0 reduce-scatter.5.cloned.1.call-update
  301.4 70.2 %all-gather.14.cloned.1.call-done = bf16[2048,448]{0,1:T(8,128)(2,1)} async-done(((bf16[128,448]{0,1:T(8,128)(2,1)}), bf16[2048,448]{0,1:T(8,128)(2,1)}) %all-gather.14.cloned.1.call-update) | async-done | bytes 1835024 | tf_op jit(solution)/shard_map/all_gather | solution.py:48
  371.5 0.0 copy-done.5
  371.5 5.1 multiply_reduce_fusion
  376.7 111.6 %all-reduce = (f32[]{:T(128)}, f32[]{:T(128)}) all-reduce(f32[]{:T(128)} %get-tuple-element.13, f32[]{:T(128)} %get-tuple-element.9), channel_id=1, replica_groups=mesh['row'=16,'col'=32] {'row','col'}, use_global_device_ids=true, to_apply=%region_3.0 | all-reduce | flops 2 | bytes 16 | tf_op jit(solution)/shard_map/psum | solution.py:79
  489.6 0.9 multiply_convert_fusion.2
  490.5 0.0 copy-start.1
  490.5 0.0 all-gather.12.cloned.1.call-done
  490.5 0.0 copy-start.6
  490.5 4.2 fusion.2
  494.7 0.0 copy-done.1
  494.7 0.0 copy-done.6
  494.7 1.9 fusion.3
  496.6 48.9 %reduce-scatter.5.cloned.1.call-done = bf16[64,512]{1,0:T(8,128)(2,1)} async-done(((bf16[2048,512]{1,0:T(8,128)(2,1)}), bf16[64,512]{1,0:T(8,128)(2,1)}) %reduce-scatter.5.cloned.1.call-update) | async-done | bytes 65552 | tf_op jit(solution)/shard_map/reduce_scatter | solution.py:72
Async XLA Ops:
  7.2 213.2 %copy-start = (bf16[512,448]{0,1:T(8,128)(2,1)S(1)}, bf16[512,448]{0,1:T(8,128)(2,1)}, u32[]{:S(2)}) copy-start(bf16[512,448]{0,1:T(8,128)(2,1)} %param.13) | copy-start | bytes 1376260
  7.2 68.9 %all-gather.6.cloned.1.call-start = ((), (), s32[]{:S(2)}) async-start(), calls=%async_computation.2 | async-start | bytes 2162688 | tf_op jit(solution)/shard_map/all_gather | solution.py:33
  7.9 135.7 %reduce-scatter.7.cloned.1.call-start = ((), (), s32[]{:S(2)}) async-start(), calls=%async_computation.8 | async-start | bytes 2228224
  81.3 63.3 %copy-start.3 = (bf16[128,448]{0,1:T(8,128)(2,1)S(1)}, bf16[128,448]{0,1:T(8,128)(2,1)}, u32[]{:S(2)}) copy-start(bf16[128,448]{0,1:T(8,128)(2,1)} %param.12) | copy-start | bytes 344068
  81.3 63.3 %copy-start.4 = (bf16[128,448]{0,1:T(8,128)(2,1)S(1)}, bf16[128,448]{0,1:T(8,128)(2,1)}, u32[]{:S(2)}) copy-start(bf16[128,448]{0,1:T(8,128)(2,1)} %param.11) | copy-start | bytes 344068
  81.4 139.0 %all-gather.8.cloned.1.call-start = ((), (), s32[]{:S(2)}) async-start(), calls=%async_computation.3 | async-start | bytes 1949696 | tf_op jit(solution)/shard_map/all_gather | solution.py:49
  145.5 150.4 %all-gather.10.cloned.1.call-start = ((), (), s32[]{:S(2)}) async-start(), calls=%async_computation.4 | async-start | bytes 1949696 | tf_op jit(solution)/shard_map/all_gather | solution.py:50
  146.1 225.4 %all-gather.14.cloned.1.call-start = ((), (), s32[]{:S(2)}) async-start(), calls=%async_computation.7 | async-start | bytes 1949696 | tf_op jit(solution)/shard_map/all_gather | solution.py:48
  146.7 343.8 %all-gather.12.cloned.1.call-start = ((), (), s32[]{:S(2)}) async-start(), calls=%async_computation.6 | async-start | bytes 2162688 | tf_op jit(solution)/shard_map/all_gather | solution.py:32
  147.3 148.7 %copy-start.2 = (bf16[512,448]{0,1:T(8,128)(2,1)S(1)}, bf16[512,448]{0,1:T(8,128)(2,1)}, u32[]{:S(2)}) copy-start(bf16[512,448]{0,1:T(8,128)(2,1)} %param.14) | copy-start | bytes 1376260
  147.3 398.2 %reduce-scatter.5.cloned.1.call-start = ((), (), s32[]{:S(2)}) async-start(), calls=%async_computation.5 | async-start | bytes 2162688 | tf_op jit(solution)/shard_map/reduce_scatter | solution.py:72
  301.3 70.2 %copy-start.5 = (bf16[2048,512]{1,0:T(8,128)(2,1)S(1)}, bf16[2048,512]{1,0:T(8,128)(2,1)}, u32[]{:S(2)}) copy-start(bf16[2048,512]{1,0:T(8,128)(2,1)} %all-gather.6.cloned.1.call-done) | copy-start | bytes 6291460
  490.5 4.2 copy-start.1
  490.5 4.2 copy-start.6
Sparse Core Ops, SparseCore 0:
  11.2 64.8 all-gather.5
  81.5 62.0 reduce-scatter.6
  146.2 74.1 all-gather.7
  222.8 73.0 all-gather.9
  298.3 73.1 all-gather.13
  374.5 66.6 all-gather.11
  446.2 99.2 reduce-scatter.4
where the time goes:
time: 554 us; the launch traced here: 553 us
  waiting for transfers between devices  395 us (71%)
  blocking collectives  112 us (20%)
  matrix products  24.2 us (4%)
  between operations  16.7 us (3%)
    psum x1, blocking collectives, shards(): lax.psum((jnp.sum(weight_vals * weight_vals), update_local), ('row', 'col'))  112 us
    all_gather x1, waiting for transfers between devices, shards(): lax.all_gather(grad_gateact, 'row', axis=0, tiled=True)  73.1 us
    all_gather x1, waiting for transfers between devices, shards(): lax.all_gather(grad_upact, 'row', axis=0, tiled=True)  70.8 us
    all_gather x1, waiting for transfers between devices, shards(): lax.all_gather(hidden, 'row', axis=0, tiled=True)  70.2 us
    all_gather x1, waiting for transfers between devices, shards(): lax.all_gather(cotangent, 'col', axis=0, tiled=True)  68.1 us
    unnamed x8, waiting for transfers between devices  64.5 us
    reduce_scatter x1, waiting for transfers between devices, shards(): lax.psum_scatter((total * scale_width).astype(jnp.bfloat16), 'col', scatt...  48.9 us
  transfers between devices with their start and end apart: 7, of which 6 were waited for; matrix products, arithmetic and copies ran while one was open for 4% of the time, Pallas kernels for 0%

commit v1 on v0

v1 whole, which is shorter than its diff:
```python
import jax
import jax.numpy as jnp
from jax import lax
from jax.experimental import pallas as pl
from jax.experimental.pallas import tpu as pltpu
from jax.sharding import PartitionSpec as P

D = 8192
FF = 14336
Z = 16
SIDE = 4
SCALE_WIDTH = float(D) ** (-0.5)
SCALE_HIDDEN = float(FF) ** (-0.5)
BF16 = jnp.bfloat16
F32 = jnp.float32
VMEM = pl.BlockSpec(memory_space=pltpu.VMEM)
SMEM = pl.BlockSpec(memory_space=pltpu.SMEM)


def params():
    return pltpu.CompilerParams(vmem_limit_bytes=48 * 1024 * 1024)


def shift_z(v, step):
    return lax.ppermute(v, "row", [(i, (i + step) % Z) for i in range(Z)])


def col_of(y, x, core):
    return ((y % SIDE) * SIDE + x % SIDE) * 2 + core


def shift_col(v, dy, dx, swap):
    pairs = []
    for y in range(SIDE):
        for x in range(SIDE):
            for core in range(2):
                pairs.append((col_of(y, x, core), col_of(y + dy, x + dx, core ^ swap)))
    return lax.ppermute(v, "col", pairs)


def shift_x(v, step):
    return shift_col(v, 0, step, 0)


def shift_y(v, step):
    return shift_col(v, step, 0, 0)


def swap_core(v):
    return shift_col(v, 0, 0, 1)


def gather_four(v, shift):
    half = v.shape[0] // 2
    before = shift(v, 1)
    after = shift(v, -1)
    far_top = shift(before[:half], 1)
    far_bottom = shift(after[half:], -1)
    return v, after, far_top, far_bottom, before


def reduce_four(parts, shift):
    half = parts[2].shape[0] // 2
    top = shift(parts[2][:half], 1)
    bottom = shift(parts[2][half:], -1)
    ahead = jnp.concatenate([add(parts[1][:half], top), parts[1][half:]], axis=0)
    behind = jnp.concatenate([parts[3][:half], add(parts[3][half:], bottom)], axis=0)
    from_before = shift(ahead, 1)
    from_after = shift(behind, -1)
    return add(parts[0], from_before, from_after)


def add(*terms):
    total = terms[0].astype(F32)
    for term in terms[1:]:
        total = total + term.astype(F32)
    return total.astype(BF16)


def ring_gather(v, far_right):
    blocks = [None] * Z
    blocks[0] = v
    right = left = v
    for step in range(1, Z // 2 + 1):
        if step < Z // 2 or far_right:
            right = shift_z(right, 1)
            blocks[(Z - step) % Z] = right
        if step < Z // 2 or not far_right:
            left = shift_z(left, -1)
            blocks[step] = left
    return blocks


def ring_reduce(parts):
    right = shift_z(parts[Z // 2], 1)
    left = shift_z(parts[Z // 2 + 1], -1)
    for step in range(2, Z // 2 + 1):
        right = shift_z(add(right, parts[Z // 2 + 1 - step]), 1)
        if step < Z // 2:
            left = shift_z(add(left, parts[Z // 2 + step]), -1)
    return add(parts[0], right, left)


def lay_out(place_ref, pieces, whole_ref):
    core = place_ref[1]
    tokens = whole_ref.shape[0]
    chip_rows = tokens // (SIDE * SIDE)
    rows = chip_rows // 2
    for owner in range(2):
        first, after, far_top, far_bottom, before = pieces[5 * owner : 5 * owner + 5]
        side = core if owner == 0 else 1 - core
        for dy in range(SIDE):
            for dx in range(SIDE):
                chip = place_ref[4 + dy * SIDE + dx]
                start = pl.multiple_of(chip * chip_rows + side * rows, rows)
                if dy == 0:
                    block = first[dx * rows : (dx + 1) * rows, :]
                elif dy == 1:
                    block = after[dx * rows : (dx + 1) * rows, :]
                elif dy == 3:
                    block = before[dx * rows : (dx + 1) * rows, :]
                elif dx < 2:
                    block = far_top[dx * rows : (dx + 1) * rows, :]
                else:
                    block = far_bottom[(dx - 2) * rows : (dx - 1) * rows, :]
                whole_ref[pl.ds(start, rows), :] = block


def hidden_partial_body(place_ref, *refs):
    pieces = refs[:10]
    weight_ref = refs[10]
    cot_ref = refs[11]
    outs = refs[12 : 12 + Z]
    hold = refs[12 + Z]
    lay_out(place_ref, pieces, cot_ref)
    tokens = cot_ref.shape[0]
    width = tokens // Z
    span = tokens // SIDE
    for part in range(SIDE):
        product = lax.dot_general(
            weight_ref[...],
            cot_ref[part * span : (part + 1) * span, :],
            (((1,), (1,)), ((), ())),
            preferred_element_type=F32,
        )
        hold[:, part * span : (part + 1) * span] = (product * SCALE_HIDDEN).astype(BF16)
    z = place_ref[0]
    for k in range(Z):
        start = pl.multiple_of(lax.rem(z + k, Z) * width, width)
        outs[k][...] = hold[:, pl.ds(start, width)]


def hidden_partial(place, pieces, weight):
    units, depth = weight.shape
    tokens = pieces[0].shape[0] * 2 * SIDE
    width = tokens // Z
    shapes = [jax.ShapeDtypeStruct((tokens, depth), BF16)]
    shapes += [jax.ShapeDtypeStruct((units, width), BF16)] * Z
    out = pl.pallas_call(
        hidden_partial_body,
        out_shape=shapes,
        in_specs=[SMEM] + [VMEM] * 11,
        out_specs=[VMEM] * (1 + Z),
        scratch_shapes=[pltpu.VMEM((units, tokens), BF16)],
        compiler_params=params(),
        cost_estimate=pl.CostEstimate(
            flops=2 * units * depth * tokens,
            bytes_accessed=2 * (2 * tokens * depth + units * depth + units * tokens),
            transcendentals=0,
        ),
        name="hidden_partial",
    )(place, *pieces, weight)
    return out[0], out[1:]


def down_body(place_ref, *refs):
    gates = refs[:Z]
    ups = refs[Z : 2 * Z]
    cot_ref, weight_ref, m_ref, v_ref = refs[2 * Z : 2 * Z + 4]
    swish_ref, slope_ref, new_m_ref, new_v_ref, update_ref, sums_ref = refs[2 * Z + 4 : 2 * Z + 10]
    hidden, product = refs[2 * Z + 10 :]
    units, width = gates[0].shape
    chunk = 64 if units % 64 == 0 else units
    z = place_ref[0]
    for k in range(Z):
        start = pl.multiple_of(lax.rem(z + k, Z) * width, width)

        @pl.loop(0, units // chunk)
        def _(i, k=k, start=start):
            rows = pl.ds(pl.multiple_of(i * chunk, chunk), chunk)
            g = gates[k][rows, :].astype(F32)
            u = ups[k][rows, :].astype(F32)
            s = jax.nn.sigmoid(g)
            swish = g * s
            hidden[rows, pl.ds(start, width)] = (swish * u).astype(BF16)
            swish_ref[rows, k * width : (k + 1) * width] = swish.astype(BF16)
            slope_ref[rows, k * width : (k + 1) * width] = (u * s * (1.0 + g * (1.0 - s))).astype(
                BF16
            )

    product[...] = lax.dot_general(
        hidden[...], cot_ref[...], (((1,), (0,)), ((), ())), preferred_element_type=F32
    )
    step = 16
    depth = product.shape[1]

    def optimizer(i, carry):
        weight_sum, update_sum = carry
        rows = pl.ds(pl.multiple_of(i * step, step), step)
        grad = product[rows, :] * SCALE_HIDDEN
        weight = weight_ref[rows, :].astype(F32)
        first = 0.9 * m_ref[rows, :].astype(F32) + 0.1 * grad
        second = 0.95 * v_ref[rows, :].astype(F32) + 0.05 * grad * grad
        update = first / (jnp.sqrt(second) + 1e-08) + 0.1 * weight
        new_m_ref[rows, :] = first.astype(BF16)
        new_v_ref[rows, :] = second.astype(BF16)
        update_ref[rows, :] = update
        return weight_sum + weight * weight, update_sum + update * update

    zero = jnp.zeros((step, depth), F32)
    weight_sum, update_sum = lax.fori_loop(0, units // step, optimizer, (zero, zero))
    sums_ref[0:1, :] = jnp.sum(weight_sum, axis=0, keepdims=True)
    sums_ref[1:2, :] = jnp.sum(update_sum, axis=0, keepdims=True)


def down_update(place, gates, ups, cotangent, weight, moment_m, moment_v):
    units, width = gates[0].shape
    tokens, depth = cotangent.shape
    shapes = [
        jax.ShapeDtypeStruct((units, tokens), BF16),
        jax.ShapeDtypeStruct((units, tokens), BF16),
        jax.ShapeDtypeStruct((units, depth), BF16),
        jax.ShapeDtypeStruct((units, depth), BF16),
        jax.ShapeDtypeStruct((units, depth), F32),
        jax.ShapeDtypeStruct((2, depth), F32),
    ]
    return pl.pallas_call(
        down_body,
        out_shape=shapes,
        in_specs=[SMEM] + [VMEM] * (2 * Z + 4),
        out_specs=[VMEM] * 6,
        scratch_shapes=[pltpu.VMEM((units, tokens), BF16), pltpu.VMEM((units, depth), F32)],
        compiler_params=params(),
        cost_estimate=pl.CostEstimate(
            flops=2 * units * depth * tokens + 30 * units * tokens,
            bytes_accessed=8 * units * tokens + 2 * tokens * depth + 14 * units * depth,
            transcendentals=units * tokens,
        ),
        name="down_update",
    )(place, *gates, *ups, cotangent, weight, moment_m, moment_v)


def input_partial_body(place_ref, *refs):
    grads = refs[:Z]
    swish_ref, slope_ref, gate_weight_ref, up_weight_ref = refs[Z : Z + 4]
    gateact_ref, upact_ref = refs[Z + 4 : Z + 6]
    mine = refs[Z + 6 : Z + 10]
    other = refs[Z + 10 : Z + 14]
    hold = refs[Z + 14]
    units, width = grads[0].shape
    tokens = gateact_ref.shape[1]
    chunk = 64 if units % 64 == 0 else units
    z, core = place_ref[0], place_ref[1]
    for k in range(Z):
        start = pl.multiple_of(lax.rem(z + k, Z) * width, width)

        @pl.loop(0, units // chunk)
        def _(i, k=k, start=start):
            rows = pl.ds(pl.multiple_of(i * chunk, chunk), chunk)
            grad = grads[k][rows, :].astype(F32)
            swish = swish_ref[rows, k * width : (k + 1) * width].astype(F32)
            slope = slope_ref[rows, k * width : (k + 1) * width].astype(F32)
            upact_ref[rows, pl.ds(start, width)] = (grad * swish).astype(BF16)
            gateact_ref[rows, pl.ds(start, width)] = (grad * slope).astype(BF16)

    span = tokens // SIDE
    contract_first = (((0,), (0,)), ((), ()))
    for part in range(SIDE):
        cols = slice(part * span, (part + 1) * span)
        product = lax.dot_general(
            gateact_ref[:, cols], gate_weight_ref[...], contract_first, preferred_element_type=F32
        )
        product = product + lax.dot_general(
            upact_ref[:, cols], up_weight_ref[...], contract_first, preferred_element_type=F32
        )
        hold[cols, :] = (product * SCALE_WIDTH).astype(BF16)
    rows = width // 2
    for dy in range(SIDE):
        for dx in range(SIDE):
            start = place_ref[4 + dy * SIDE + dx] * width
            own = pl.ds(pl.multiple_of(start + core * rows, rows), rows)
            their = pl.ds(pl.multiple_of(start + (1 - core) * rows, rows), rows)
            mine[dy][dx * rows : (dx + 1) * rows, :] = hold[own, :]
            other[dy][dx * rows : (dx + 1) * rows, :] = hold[their, :]


def input_partial(place, grads, swish, slope, gate_weight, up_weight):
    units, width = grads[0].shape
    depth = gate_weight.shape[1]
    tokens = width * Z
    quarter = jax.ShapeDtypeStruct((tokens // 8, depth), BF16)
    acts = jax.ShapeDtypeStruct((units, tokens), BF16)
    out = pl.pallas_call(
        input_partial_body,
        out_shape=[acts, acts] + [quarter] * 8,
        in_specs=[SMEM] + [VMEM] * (Z + 4),
        out_specs=[VMEM] * 10,
        scratch_shapes=[pltpu.VMEM((tokens, depth), BF16)],
        compiler_params=params(),
        cost_estimate=pl.CostEstimate(
            flops=4 * units * depth * tokens,
            bytes_accessed=10 * units * tokens + 2 * tokens * depth + 4 * units * depth,
            transcendentals=0,
        ),
        name="input_partial",
    )(place, *grads, swish, slope, gate_weight, up_weight)
    return out[0], out[1], out[2:6], out[6:10]


def gather_col(v):
    first, after, far_top, far_bottom, before = gather_four(v, shift_x)
    stack = jnp.concatenate([first, after, far_top, far_bottom, before], axis=0)
    own = gather_four(stack, shift_y)
    return list(own) + [swap_core(piece) for piece in own]


def shards(
    tokens, cotangent, gate_pre, up_act, gate_weight, up_weight, down_weight, moment_m, moment_v
):
    z = lax.axis_index("row")
    col = lax.axis_index("col")
    core, chip = col % 2, col // 2
    y, x = chip // SIDE, chip % SIDE
    offsets = jnp.arange(SIDE)
    chips = ((y + offsets) % SIDE)[:, None] * SIDE + ((x + offsets) % SIDE)[None, :]
    place = jnp.concatenate(
        [jnp.stack([z, core, y, x]).astype(jnp.int32), chips.reshape(-1).astype(jnp.int32)]
    )

    pieces = gather_col(cotangent)
    gates = ring_gather(gate_pre.T, True)
    ups = ring_gather(up_act.T, False)
    cotangent_all, partials = hidden_partial(place, pieces, down_weight)
    tokens, _ = lax.optimization_barrier((tokens, pieces[4]))
    tokens_all = lax.all_gather(tokens, "col", axis=0, tiled=True)

    grad_hidden = ring_reduce(partials)
    grads = ring_gather(grad_hidden, True)

    swish, slope, new_m, new_v, update, sums = down_update(
        place, gates, ups, cotangent_all, down_weight, moment_m, moment_v
    )
    sums = jnp.sum(sums, axis=1).reshape(1, 2)
    sums = jnp.sum(lax.all_gather(sums, "col", axis=0, tiled=True), axis=0, keepdims=True)
    sums = jnp.sum(lax.all_gather(sums, "row", axis=0, tiled=True), axis=0)
    trust_ratio = jnp.sqrt(sums[0]) / jnp.sqrt(sums[1] + 1e-06)
    step_down = (trust_ratio * update).astype(BF16)

    gateact, upact, mine, other = input_partial(
        place, grads, swish, slope, gate_weight.T, up_weight.T
    )
    merged = [add(a, swap_core(b)) for a, b in zip(mine, other)]
    quarter = reduce_four(merged, shift_y)
    rows = quarter.shape[0] // SIDE
    grad_input = reduce_four([quarter[k * rows : (k + 1) * rows] for k in range(SIDE)], shift_x)

    contract = (((1,), (0,)), ((), ()))
    grad_gate = lax.dot_general(gateact, tokens_all, contract, preferred_element_type=F32)
    grad_up = lax.dot_general(upact, tokens_all, contract, preferred_element_type=F32)
    return (
        grad_input,
        (grad_gate * SCALE_WIDTH).astype(BF16).T,
        (grad_up * SCALE_WIDTH).astype(BF16).T,
        new_m,
        new_v,
        step_down,
        trust_ratio,
    )


def solution(mesh):
    in_specs = (
        P("col", "row"),
        P("col", "row"),
        P("row", "col"),
        P("row", "col"),
        P("row", "col"),
        P("row", "col"),
        P("col", "row"),
        P("col", "row"),
        P("col", "row"),
    )
    out_specs = (
        P("col", "row"),
        P("row", "col"),
        P("row", "col"),
        P("col", "row"),
        P("col", "row"),
        P("col", "row"),
        P(),
    )
    return jax.shard_map(shards, mesh=mesh, in_specs=in_specs, out_specs=out_specs, check_vma=False)
```

time: 554 us -> 529 us (0.955)
  the two profiles are of different devices: /device:TPU:1 before, /device:TPU:6 now
where the time goes in v1:
time: 529 us; the launch traced here: 526 us
  starting transfers between devices  280 us (53%)
  blocking collectives  79.9 us (15%)
  waiting for transfers between devices  69.7 us (13%)
  local copies, waits for them, and re-layouts  47.2 us (9%)
  Pallas kernels  21.3 us (4%)
  between operations  19.7 us (4%)
  matrix products  5.53 us (1%)
    ppermute x60, starting transfers between devices, shift_z(): return lax.ppermute(v, 'row', [(i, (i + step) % Z) for i in range(Z)])  191 us
    ppermute x25, starting transfers between devices, shift_col(): return lax.ppermute(v, 'col', pairs)  89.4 us
    unnamed x2, blocking collectives  79.9 us
    ppermute x60, waiting for transfers between devices, shift_z(): return lax.ppermute(v, 'row', [(i, (i + step) % Z) for i in range(Z)])  52.9 us
    unnamed x172, local copies, waits for them, and re-layouts  46.2 us
    ppermute x25, waiting for transfers between devices, shift_col(): return lax.ppermute(v, 'col', pairs)  16.8 us
  transfers between devices with their start and end apart: 86, of which 18 were waited for; matrix products, arithmetic and copies ran while one was open for 1% of the time, Pallas kernels for 4%

profile of v1, /device:TPU:6, one launch (start us, length us, event | category | flops | bytes accessed | tf_op | source)
XLA Modules:
  0.0 526.0 jit_solution(9921176897747069046)
XLA Ops:
  7.2 2.7 collective-permute-start
  10.0 6.9 %collective-permute-start.1 = (bf16[64,512]{1,0:T(8,128)(2,1)}, bf16[64,512]{1,0:T(8,128)(2,1)S(1)}, u32[]{:S(2)}, u32[]{:S(2)}) collective-permute-start(bf16[64,512]{1,0:T(8,128)(2,1)} %param.10), channel_id=1, source_target_pairs={{0,2},{1,3},{2,4},{3,5},{4,6},{5,7},{6,0},{7,1},{8,10},{9,11},{10,... | collective-permute-start | bytes 196616 | tf_op jit(solution)/shard_map/ppermute | solution.py:38
  19.1 5.4 %collective-permute-start.2 = (bf16[32,512]{1,0:T(8,128)(2,1)S(1)}, bf16[32,512]{1,0:T(8,128)(2,1)S(1)}, u32[]{:S(2)}, u32[]{:S(2)}) collective-permute-start(bf16[32,512]{1,0:T(8,128)(2,1)S(1)} %slice.85), channel_id=1, source_target_pairs={{0,2},{1,3},{2,4},{3,5},{4,6},{5,7},{6,0},{7,1},{8,10},{9,11},{10,... | collective-permute-start | bytes 98312 | tf_op jit(solution)/shard_map/ppermute | solution.py:38
  26.5 5.1 collective-permute-done.3
  33.5 5.1 collective-permute-start.4
  38.6 3.4 collective-permute-done.5.refs_4_
  44.0 5.3 %collective-permute-start.7 = (bf16[128,512]{1,0:T(8,128)(2,1)S(1)}, bf16[128,512]{1,0:T(8,128)(2,1)S(1)}, u32[]{:S(2)}, u32[]{:S(2)}) collective-permute-start(bf16[128,512]{1,0:T(8,128)(2,1)S(1)} %slice.88), channel_id=1, source_target_pairs={{0,24},{1,25},{2,26},{3,27},{4,28},{5,29},{6,30},{7,31},{8,0},{9,1... | collective-permute-start | bytes 393224 | tf_op jit(solution)/shard_map/ppermute | solution.py:38
  51.2 2.4 collective-permute-start.12
  55.6 2.4 collective-permute-start.10
  63.2 3.7 hidden_partial.1
  69.0 7.6 %collective-permute-start.43 = (bf16[448,128]{1,0:T(8,128)(2,1)S(1)}, bf16[448,128]{1,0:T(8,128)(2,1)S(1)}, u32[]{:S(2)}, u32[]{:S(2)}) collective-permute-start(bf16[448,128]{1,0:T(8,128)(2,1)S(1)} %bitcast.16), channel_id=1, source_target_pairs={{0,480},{32,0},{64,32},{96,64},{128,96},{160,128},{192,160},{224,1... | collective-permute-start | bytes 344072 | tf_op jit(solution)/shard_map/ppermute | solution.py:25
  76.6 3.9 collective-permute-start.58
  84.4 5.1 collective-permute-start.21
  93.8 6.3 %collective-permute-done.14 = bf16[448,128]{1,0:T(8,128)(2,1)S(1)} collective-permute-done((bf16[448,128]{1,0:T(8,128)(2,1)S(1)}, bf16[448,128]{1,0:T(8,128)(2,1)S(1)}, u32[]{:S(2)}, u32[]{:S(2)}) %collective-permute-start.14) | collective-permute-done | bytes 114720 | tf_op jit(solution)/shard_map/ppermute | solution.py:25
  100.2 3.9 collective-permute-start.22
  104.1 2.7 collective-permute-done.22
  108.9 5.9 %collective-permute-done.15 = bf16[448,128]{1,0:T(8,128)(2,1)S(1)} collective-permute-done((bf16[448,128]{1,0:T(8,128)(2,1)S(1)}, bf16[448,128]{1,0:T(8,128)(2,1)S(1)}, u32[]{:S(2)}, u32[]{:S(2)}) %collective-permute-start.15) | collective-permute-done | bytes 114720 | tf_op jit(solution)/shard_map/ppermute | solution.py:25
  114.7 3.9 collective-permute-start.23
  118.7 2.7 collective-permute-done.23
  123.4 5.9 %collective-permute-done.16 = bf16[448,128]{1,0:T(8,128)(2,1)S(1)} collective-permute-done((bf16[448,128]{1,0:T(8,128)(2,1)S(1)}, bf16[448,128]{1,0:T(8,128)(2,1)S(1)}, u32[]{:S(2)}, u32[]{:S(2)}) %collective-permute-start.16) | collective-permute-done | bytes 114720 | tf_op jit(solution)/shard_map/ppermute | solution.py:25
  129.3 3.9 collective-permute-start.24
  133.3 2.7 collective-permute-done.24
  137.9 5.9 %collective-permute-done.17 = bf16[448,128]{1,0:T(8,128)(2,1)S(1)} collective-permute-done((bf16[448,128]{1,0:T(8,128)(2,1)S(1)}, bf16[448,128]{1,0:T(8,128)(2,1)S(1)}, u32[]{:S(2)}, u32[]{:S(2)}) %collective-permute-start.17) | collective-permute-done | bytes 114720 | tf_op jit(solution)/shard_map/ppermute | solution.py:25
  143.9 3.9 collective-permute-start.25
  147.8 2.7 collective-permute-done.25
  152.5 6.3 %collective-permute-done.18 = bf16[448,128]{1,0:T(8,128)(2,1)S(1)} collective-permute-done((bf16[448,128]{1,0:T(8,128)(2,1)S(1)}, bf16[448,128]{1,0:T(8,128)(2,1)S(1)}, u32[]{:S(2)}, u32[]{:S(2)}) %collective-permute-start.18) | collective-permute-done | bytes 114720 | tf_op jit(solution)/shard_map/ppermute | solution.py:25
  158.8 4.3 collective-permute-start.26
  163.1 3.3 collective-permute-done.26
  168.4 5.9 %collective-permute-done.19 = bf16[448,128]{1,0:T(8,128)(2,1)S(1)} collective-permute-done((bf16[448,128]{1,0:T(8,128)(2,1)S(1)}, bf16[448,128]{1,0:T(8,128)(2,1)S(1)}, u32[]{:S(2)}, u32[]{:S(2)}) %collective-permute-start.19) | collective-permute-done | bytes 114720 | tf_op jit(solution)/shard_map/ppermute | solution.py:25
  174.3 3.9 collective-permute-start.27
  180.2 5.1 collective-permute-start.59
  187.3 3.9 collective-permute-start.67
  195.2 5.1 collective-permute-start.60
  200.3 3.9 collective-permute-start.45
  206.2 5.1 collective-permute-start.28
  216.5 5.1 collective-permute-start.61
  222.3 3.9 collective-permute-start.46
  229.4 3.9 collective-permute-start.37
  239.1 5.1 collective-permute-start.62
  244.9 3.9 collective-permute-start.30
  252.0 5.1 collective-permute-start.47
  263.0 5.1 collective-permute-start.31
  271.3 5.1 collective-permute-start.63
  277.1 2.7 collective-permute-start.48
  280.4 3.1 collective-permute-start.71
  284.2 3.9 collective-permute-start.32
  293.9 5.1 collective-permute-start.64
  299.7 3.9 collective-permute-start.49
  307.0 3.7 collective-permute-start.41
  317.2 5.1 collective-permute-start.65
  323.0 3.9 collective-permute-start.34
  350.6 9.2 %down_update.1 = (bf16[448,2048]{1,0:T(8,128)(2,1)}, bf16[448,2048]{1,0:T(8,128)(2,1)}, bf16[448,512]{1,0:T(8,128)(2,1)}, bf16[448,512]{1,0:T(8,128)(2,1)}, f32[...) custom-call(s32[20]{0:T(128)S(1)} %copy-done.53, bf16[448,128]{1,0:T(8,128)(2,1)S(1)} %bitcast.17, ...), custom_call_target="tpu_custom_call" | custom-call | flops 967049216 | bytes 12648448 | tf_op jit(solution)/shard_map/down_update/pallas_call | solution.py:237
  360.5 8.5 %input_partial.1 = (bf16[448,2048]{1,0:T(8,128)(2,1)}, bf16[448,2048]{1,0:T(8,128)(2,1)}, bf16[256,512]{1,0:T(8,128)(2,1)S(1)}, bf16[256,512]{1,0:T(8,128)(2,1)S...) custom-call(s32[20]{0:T(128)S(1)} %copy-done.53, ...), custom_call_target="tpu_custom_call" | custom-call | flops 1879048192 | bytes 12189696 | tf_op jit(solution)/shard_map/input_partial/pallas_call | solution.py:303
  370.9 2.4 collective-permute-start.74
  375.3 2.4 collective-permute-start.73
  379.8 5.1 collective-permute-start.79
  388.4 5.1 collective-permute-start.80
  397.7 48.8 %all-reduce = f32[64]{0:T(128)S(1)} all-reduce(f32[64]{0:T(128)S(1)} %dynamic-update-slice), channel_id=2, replica_groups=mesh['row'=16,'col'=32] {'col'}, use_global_device_ids=true, to_apply=%add | all-reduce | flops 64 | bytes 512
  446.9 31.1 %all-reduce.1 = f32[32]{0:T(128)S(1)} all-reduce(f32[32]{0:T(128)S(1)} %dynamic-update-slice.1), channel_id=3, replica_groups=mesh['row'=16,'col'=32] {'row'}, use_global_device_ids=true, to_apply=%add.1 | all-reduce | flops 32 | bytes 256
  478.3 17.0 %collective-permute-start.81 = (bf16[32,512]{1,0:T(8,128)(2,1)S(1)}, bf16[32,512]{1,0:T(8,128)(2,1)S(1)}, u32[]{:S(2)}, u32[]{:S(2)}) collective-permute-start(bf16[32,512]{1,0:T(8,128)(2,1)S(1)} %get-tuple-element.77), channel_id=1, source_target_pairs={{0,2},{1,3},{2,4},{3,5},{4,6},{5,7},{6,0},{7,1},{8,10},{9,11},{10,... | collective-permute-start | bytes 98312 | tf_op jit(solution)/shard_map/ppermute | solution.py:38
  499.3 3.1 collective-permute-done.83
  504.5 3.8 collective-permute-start.84
  509.2 2.7 collective-permute-done.84
  512.5 3.6 fusion
  (334 shorter events, 138.0 us)
Async XLA Ops:
  7.2 505.4 %all-gather.4.cloned.1.call-start = ((), (), s32[]{:S(2)}) async-start(), calls=%async_computation | async-start | bytes 2162688 | tf_op jit(solution)/shard_map/all_gather | solution.py:345
  7.2 17.3 %collective-permute-start = (bf16[64,512]{1,0:T(8,128)(2,1)}, bf16[64,512]{1,0:T(8,128)(2,1)S(1)}, u32[]{:S(2)}, u32[]{:S(2)}) collective-permute-start(bf16[64,512]{1,0:T(8,128)(2,1)} %param.10), channel_id=1, source_target_pairs={{0,6},{1,7},{2,0},{3,1},{4,2},{5,3},{6,4},{7,5},{8,14},{9,15},{10,... | collective-permute-start | bytes 196616 | tf_op jit(solution)/shard_map/ppermute | solution.py:38
  10.0 9.2 %collective-permute-start.1 = (bf16[64,512]{1,0:T(8,128)(2,1)}, bf16[64,512]{1,0:T(8,128)(2,1)S(1)}, u32[]{:S(2)}, u32[]{:S(2)}) collective-permute-start(bf16[64,512]{1,0:T(8,128)(2,1)} %param.10), channel_id=1, source_target_pairs={{0,2},{1,3},{2,4},{3,5},{4,6},{5,7},{6,0},{7,1},{8,10},{9,11},{10,... | collective-permute-start | bytes 196616 | tf_op jit(solution)/shard_map/ppermute | solution.py:38
  31.5 10.4 %collective-permute-start.5 = (bf16[256,512]{1,0:T(8,128)(2,1)S(1)}, bf16[256,512]{1,0:T(8,128)(2,1)S(1)}, u32[]{:S(2)}, u32[]{:S(2)}) collective-permute-start(bf16[256,512]{1,0:T(8,128)(2,1)S(1)} %constant_dynamic-update-slice_fusion.refs_0_), channel_id=1, source_target_pairs={{0,8},{1,9},{2,10},{3,11},{4,12},{5,13},{6,14},{7,15},{8,16},{9,17... | collective-permute-start | bytes 786440 | tf_op jit(solution)/shard_map/ppermute | solution.py:38
  33.5 10.4 %collective-permute-start.4 = (bf16[256,512]{1,0:T(8,128)(2,1)S(1)}, bf16[256,512]{1,0:T(8,128)(2,1)S(1)}, u32[]{:S(2)}, u32[]{:S(2)}) collective-permute-start(bf16[256,512]{1,0:T(8,128)(2,1)S(1)} %constant_dynamic-update-slice_fusion.refs_0_), channel_id=1, source_target_pairs={{0,24},{1,25},{2,26},{3,27},{4,28},{5,29},{6,30},{7,31},{8,0},{9,1... | collective-permute-start | bytes 786440 | tf_op jit(solution)/shard_map/ppermute | solution.py:38
  42.0 13.6 %collective-permute-start.6 = (bf16[128,512]{1,0:T(8,128)(2,1)S(1)}, bf16[128,512]{1,0:T(8,128)(2,1)S(1)}, u32[]{:S(2)}, u32[]{:S(2)}) collective-permute-start(bf16[128,512]{1,0:T(8,128)(2,1)S(1)} %slice.87), channel_id=1, source_target_pairs={{0,8},{1,9},{2,10},{3,11},{4,12},{5,13},{6,14},{7,15},{8,16},{9,17... | collective-permute-start | bytes 393224 | tf_op jit(solution)/shard_map/ppermute | solution.py:38
  44.0 14.1 %collective-permute-start.7 = (bf16[128,512]{1,0:T(8,128)(2,1)S(1)}, bf16[128,512]{1,0:T(8,128)(2,1)S(1)}, u32[]{:S(2)}, u32[]{:S(2)}) collective-permute-start(bf16[128,512]{1,0:T(8,128)(2,1)S(1)} %slice.88), channel_id=1, source_target_pairs={{0,24},{1,25},{2,26},{3,27},{4,28},{5,29},{6,30},{7,31},{8,0},{9,1... | collective-permute-start | bytes 393224 | tf_op jit(solution)/shard_map/ppermute | solution.py:38
  49.3 10.9 %collective-permute-start.8 = (bf16[256,512]{1,0:T(8,128)(2,1)S(1)}, bf16[256,512]{1,0:T(8,128)(2,1)S(1)}, u32[]{:S(2)}, u32[]{:S(2)}) collective-permute-start(bf16[256,512]{1,0:T(8,128)(2,1)S(1)} %constant_dynamic-update-slice_fusion.refs_0_), channel_id=1, source_target_pairs={{0,1},{1,0},{2,3},{3,2},{4,5},{5,4},{6,7},{7,6},{8,9},{9,8},{10,11... | collective-permute-start | bytes 786440 | tf_op jit(solution)/shard_map/ppermute | solution.py:38
  51.2 10.9 %collective-permute-start.12 = (bf16[256,512]{1,0:T(8,128)(2,1)S(1)}, bf16[256,512]{1,0:T(8,128)(2,1)S(1)}, u32[]{:S(2)}, u32[]{:S(2)}) collective-permute-start(bf16[256,512]{1,0:T(8,128)(2,1)S(1)} %collective-permute-done.5.refs_4_), channel_id=1, source_target_pairs={{0,1},{1,0},{2,3},{3,2},{4,5},{5,4},{6,7},{7,6},{8,9},{9,8},{10,11... | collective-permute-start | bytes 786440 | tf_op jit(solution)/shard_map/ppermute | solution.py:38
  60.2 22.2 %collective-permute-start.50 = (bf16[448,128]{1,0:T(8,128)(2,1)}, bf16[448,128]{1,0:T(8,128)(2,1)S(1)}, u32[]{:S(2)}, u32[]{:S(2)}) collective-permute-start(bf16[448,128]{1,0:T(8,128)(2,1)} %bitcast.15), channel_id=1, source_target_pairs={{0,32},{32,64},{64,96},{96,128},{128,160},{160,192},{192,224},{224... | collective-permute-start | bytes 344072 | tf_op jit(solution)/shard_map/ppermute | solution.py:25
  66.9 17.5 %collective-permute-start.13 = (bf16[448,128]{1,0:T(8,128)(2,1)S(1)}, bf16[448,128]{1,0:T(8,128)(2,1)S(1)}, u32[]{:S(2)}, u32[]{:S(2)}) collective-permute-start(bf16[448,128]{1,0:T(8,128)(2,1)S(1)} %get-tuple-element.42), channel_id=1, source_target_pairs={{0,32},{32,64},{64,96},{96,128},{128,160},{160,192},{192,224},{224... | collective-permute-start | bytes 344072 | tf_op jit(solution)/shard_map/ppermute | solution.py:25
  69.0 111.2 %collective-permute-start.43 = (bf16[448,128]{1,0:T(8,128)(2,1)S(1)}, bf16[448,128]{1,0:T(8,128)(2,1)S(1)}, u32[]{:S(2)}, u32[]{:S(2)}) collective-permute-start(bf16[448,128]{1,0:T(8,128)(2,1)S(1)} %bitcast.16), channel_id=1, source_target_pairs={{0,480},{32,0},{64,32},{96,64},{128,96},{160,128},{192,160},{224,1... | collective-permute-start | bytes 344072 | tf_op jit(solution)/shard_map/ppermute | solution.py:25
  76.6 101.7 %collective-permute-start.58 = (bf16[448,128]{1,0:T(8,128)(2,1)S(1)}, bf16[448,128]{1,0:T(8,128)(2,1)S(1)}, u32[]{:S(2)}, u32[]{:S(2)}) collective-permute-start(bf16[448,128]{1,0:T(8,128)(2,1)S(1)} %bitcast.18), channel_id=1, source_target_pairs={{0,480},{32,0},{64,32},{96,64},{128,96},{160,128},{192,160},{224,1... | collective-permute-start | bytes 344072 | tf_op jit(solution)/shard_map/ppermute | solution.py:25
  80.5 104.8 %collective-permute-start.66 = (bf16[448,128]{1,0:T(8,128)(2,1)S(1)}, bf16[448,128]{1,0:T(8,128)(2,1)S(1)}, u32[]{:S(2)}, u32[]{:S(2)}) collective-permute-start(bf16[448,128]{1,0:T(8,128)(2,1)S(1)} %bitcast.19), channel_id=1, source_target_pairs={{0,32},{32,64},{64,96},{96,128},{128,160},{160,192},{192,224},{224... | collective-permute-start | bytes 344072 | tf_op jit(solution)/shard_map/ppermute | solution.py:25
  82.5 104.8 %collective-permute-start.51 = (bf16[448,128]{1,0:T(8,128)(2,1)S(1)}, bf16[448,128]{1,0:T(8,128)(2,1)S(1)}, u32[]{:S(2)}, u32[]{:S(2)}) collective-permute-start(bf16[448,128]{1,0:T(8,128)(2,1)S(1)} %collective-permute-done.50.refs_15_), channel_id=1, source_target_pairs={{0,32},{32,64},{64,96},{96,128},{128,160},{160,192},{192,224},{224... | collective-permute-start | bytes 344072 | tf_op jit(solution)/shard_map/ppermute | solution.py:25
  174.3 16.9 %collective-permute-start.27 = (bf16[448,128]{1,0:T(8,128)(2,1)S(1)}, bf16[448,128]{1,0:T(8,128)(2,1)S(1)}, u32[]{:S(2)}, u32[]{:S(2)}) collective-permute-start(bf16[448,128]{1,0:T(8,128)(2,1)S(1)} %add_convert_fusion.8), channel_id=1, source_target_pairs={{0,480},{32,0},{64,32},{96,64},{128,96},{160,128},{192,160},{224,1... | collective-permute-start | bytes 344072 | tf_op jit(solution)/shard_map/ppermute | solution.py:25
  178.3 14.9 %collective-permute-start.20 = (bf16[448,128]{1,0:T(8,128)(2,1)S(1)}, bf16[448,128]{1,0:T(8,128)(2,1)S(1)}, u32[]{:S(2)}, u32[]{:S(2)}) collective-permute-start(bf16[448,128]{1,0:T(8,128)(2,1)S(1)} %add_convert_fusion.14), channel_id=1, source_target_pairs={{0,32},{32,64},{64,96},{96,128},{128,160},{160,192},{192,224},{224... | collective-permute-start | bytes 344072 | tf_op jit(solution)/shard_map/ppermute | solution.py:25
  180.2 15.0 %collective-permute-start.59 = (bf16[448,128]{1,0:T(8,128)(2,1)S(1)}, bf16[448,128]{1,0:T(8,128)(2,1)S(1)}, u32[]{:S(2)}, u32[]{:S(2)}) collective-permute-start(bf16[448,128]{1,0:T(8,128)(2,1)S(1)} %collective-permute-done.58.refs_17_), channel_id=1, source_target_pairs={{0,480},{32,0},{64,32},{96,64},{128,96},{160,128},{192,160},{224,1... | collective-permute-start | bytes 344072 | tf_op jit(solution)/shard_map/ppermute | solution.py:25
  185.4 15.0 %collective-permute-start.44 = (bf16[448,128]{1,0:T(8,128)(2,1)S(1)}, bf16[448,128]{1,0:T(8,128)(2,1)S(1)}, u32[]{:S(2)}, u32[]{:S(2)}) collective-permute-start(bf16[448,128]{1,0:T(8,128)(2,1)S(1)} %collective-permute-done.43.refs_1_), channel_id=1, source_target_pairs={{0,480},{32,0},{64,32},{96,64},{128,96},{160,128},{192,160},{224,1... | collective-permute-start | bytes 344072 | tf_op jit(solution)/shard_map/ppermute | solution.py:25
  187.3 17.0 %collective-permute-start.67 = (bf16[448,128]{1,0:T(8,128)(2,1)S(1)}, bf16[448,128]{1,0:T(8,128)(2,1)S(1)}, u32[]{:S(2)}, u32[]{:S(2)}) collective-permute-start(bf16[448,128]{1,0:T(8,128)(2,1)S(1)} %collective-permute-done.66.refs_31_), channel_id=1, source_target_pairs={{0,32},{32,64},{64,96},{96,128},{128,160},{160,192},{192,224},{224... | collective-permute-start | bytes 344072 | tf_op jit(solution)/shard_map/ppermute | solution.py:25
  191.2 15.0 %collective-permute-start.52 = (bf16[448,128]{1,0:T(8,128)(2,1)S(1)}, bf16[448,128]{1,0:T(8,128)(2,1)S(1)}, u32[]{:S(2)}, u32[]{:S(2)}) collective-permute-start(bf16[448,128]{1,0:T(8,128)(2,1)S(1)} %collective-permute-done.51.refs_14_), channel_id=1, source_target_pairs={{0,32},{32,64},{64,96},{96,128},{128,160},{160,192},{192,224},{224... | collective-permute-start | bytes 344072 | tf_op jit(solution)/shard_map/ppermute | solution.py:25
  193.2 18.8 %collective-permute-start.35 = (bf16[448,128]{1,0:T(8,128)(2,1)S(1)}, bf16[448,128]{1,0:T(8,128)(2,1)S(1)}, u32[]{:S(2)}, u32[]{:S(2)}) collective-permute-start(bf16[448,128]{1,0:T(8,128)(2,1)S(1)} %add_convert_fusion.7.refs_0_), channel_id=1, source_target_pairs={{0,32},{32,64},{64,96},{96,128},{128,160},{160,192},{192,224},{224... | collective-permute-start | bytes 344072 | tf_op jit(solution)/shard_map/ppermute | solution.py:25
  195.2 19.4 %collective-permute-start.60 = (bf16[448,128]{1,0:T(8,128)(2,1)S(1)}, bf16[448,128]{1,0:T(8,128)(2,1)S(1)}, u32[]{:S(2)}, u32[]{:S(2)}) collective-permute-start(bf16[448,128]{1,0:T(8,128)(2,1)S(1)} %collective-permute-done.59.refs_18_), channel_id=1, source_target_pairs={{0,480},{32,0},{64,32},{96,64},{128,96},{160,128},{192,160},{224,1... | collective-permute-start | bytes 344072 | tf_op jit(solution)/shard_map/ppermute | solution.py:25
  200.3 16.2 %collective-permute-start.45 = (bf16[448,128]{1,0:T(8,128)(2,1)S(1)}, bf16[448,128]{1,0:T(8,128)(2,1)S(1)}, u32[]{:S(2)}, u32[]{:S(2)}) collective-permute-start(bf16[448,128]{1,0:T(8,128)(2,1)S(1)} %collective-permute-done.44.refs_2_), channel_id=1, source_target_pairs={{0,480},{32,0},{64,32},{96,64},{128,96},{160,128},{192,160},{224,1... | collective-permute-start | bytes 344072 | tf_op jit(solution)/shard_map/ppermute | solution.py:25
  204.3 18.0 %collective-permute-start.68 = (bf16[448,128]{1,0:T(8,128)(2,1)S(1)}, bf16[448,128]{1,0:T(8,128)(2,1)S(1)}, u32[]{:S(2)}, u32[]{:S(2)}) collective-permute-start(bf16[448,128]{1,0:T(8,128)(2,1)S(1)} %collective-permute-done.67.refs_30_), channel_id=1, source_target_pairs={{0,32},{32,64},{64,96},{96,128},{128,160},{160,192},{192,224},{224... | collective-permute-start | bytes 344072 | tf_op jit(solution)/shard_map/ppermute | solution.py:25
  206.2 20.7 %collective-permute-start.28 = (bf16[448,128]{1,0:T(8,128)(2,1)S(1)}, bf16[448,128]{1,0:T(8,128)(2,1)S(1)}, u32[]{:S(2)}, u32[]{:S(2)}) collective-permute-start(bf16[448,128]{1,0:T(8,128)(2,1)S(1)} %add_convert_fusion.7.refs_0_), channel_id=1, source_target_pairs={{0,480},{32,0},{64,32},{96,64},{128,96},{160,128},{192,160},{224,1... | collective-permute-start | bytes 344072 | tf_op jit(solution)/shard_map/ppermute | solution.py:25
  212.0 17.4 %collective-permute-start.36 = (bf16[448,128]{1,0:T(8,128)(2,1)S(1)}, bf16[448,128]{1,0:T(8,128)(2,1)S(1)}, u32[]{:S(2)}, u32[]{:S(2)}) collective-permute-start(bf16[448,128]{1,0:T(8,128)(2,1)S(1)} %collective-permute-done.35.refs_15_), channel_id=1, source_target_pairs={{0,32},{32,64},{64,96},{96,128},{128,160},{160,192},{192,224},{224... | collective-permute-start | bytes 344072 | tf_op jit(solution)/shard_map/ppermute | solution.py:25
  214.6 19.4 %collective-permute-start.53 = (bf16[448,128]{1,0:T(8,128)(2,1)S(1)}, bf16[448,128]{1,0:T(8,128)(2,1)S(1)}, u32[]{:S(2)}, u32[]{:S(2)}) collective-permute-start(bf16[448,128]{1,0:T(8,128)(2,1)S(1)} %collective-permute-done.52.refs_13_), channel_id=1, source_target_pairs={{0,32},{32,64},{64,96},{96,128},{128,160},{160,192},{192,224},{224... | collective-permute-start | bytes 344072 | tf_op jit(solution)/shard_map/ppermute | solution.py:25
  216.5 20.1 %collective-permute-start.61 = (bf16[448,128]{1,0:T(8,128)(2,1)S(1)}, bf16[448,128]{1,0:T(8,128)(2,1)S(1)}, u32[]{:S(2)}, u32[]{:S(2)}) collective-permute-start(bf16[448,128]{1,0:T(8,128)(2,1)S(1)} %collective-permute-done.60.refs_19_), channel_id=1, source_target_pairs={{0,480},{32,0},{64,32},{96,64},{128,96},{160,128},{192,160},{224,1... | collective-permute-start | bytes 344072 | tf_op jit(solution)/shard_map/ppermute | solution.py:25
  222.3 16.8 %collective-permute-start.46 = (bf16[448,128]{1,0:T(8,128)(2,1)S(1)}, bf16[448,128]{1,0:T(8,128)(2,1)S(1)}, u32[]{:S(2)}, u32[]{:S(2)}) collective-permute-start(bf16[448,128]{1,0:T(8,128)(2,1)S(1)} %collective-permute-done.45.refs_3_), channel_id=1, source_target_pairs={{0,480},{32,0},{64,32},{96,64},{128,96},{160,128},{192,160},{224,1... | collective-permute-start | bytes 344072 | tf_op jit(solution)/shard_map/ppermute | solution.py:25
  226.9 18.0 %collective-permute-start.29 = (bf16[448,128]{1,0:T(8,128)(2,1)S(1)}, bf16[448,128]{1,0:T(8,128)(2,1)S(1)}, u32[]{:S(2)}, u32[]{:S(2)}) collective-permute-start(bf16[448,128]{1,0:T(8,128)(2,1)S(1)} %collective-permute-done.28.refs_1_), channel_id=1, source_target_pairs={{0,480},{32,0},{64,32},{96,64},{128,96},{160,128},{192,160},{224,1... | collective-permute-start | bytes 344072 | tf_op jit(solution)/shard_map/ppermute | solution.py:25
  229.4 20.0 %collective-permute-start.37 = (bf16[448,128]{1,0:T(8,128)(2,1)S(1)}, bf16[448,128]{1,0:T(8,128)(2,1)S(1)}, u32[]{:S(2)}, u32[]{:S(2)}) collective-permute-start(bf16[448,128]{1,0:T(8,128)(2,1)S(1)} %collective-permute-done.36.refs_14_), channel_id=1, source_target_pairs={{0,32},{32,64},{64,96},{96,128},{128,160},{160,192},{192,224},{224... | collective-permute-start | bytes 344072 | tf_op jit(solution)/shard_map/ppermute | solution.py:25
  234.0 18.0 %collective-permute-start.69 = (bf16[448,128]{1,0:T(8,128)(2,1)S(1)}, bf16[448,128]{1,0:T(8,128)(2,1)S(1)}, u32[]{:S(2)}, u32[]{:S(2)}) collective-permute-start(bf16[448,128]{1,0:T(8,128)(2,1)S(1)} %collective-permute-done.68.refs_29_), channel_id=1, source_target_pairs={{0,32},{32,64},{64,96},{96,128},{128,160},{160,192},{192,224},{224... | collective-permute-start | bytes 344072 | tf_op jit(solution)/shard_map/ppermute | solution.py:25
  236.6 21.3 %collective-permute-start.54 = (bf16[448,128]{1,0:T(8,128)(2,1)S(1)}, bf16[448,128]{1,0:T(8,128)(2,1)S(1)}, u32[]{:S(2)}, u32[]{:S(2)}) collective-permute-start(bf16[448,128]{1,0:T(8,128)(2,1)S(1)} %collective-permute-done.53.refs_12_), channel_id=1, source_target_pairs={{0,32},{32,64},{64,96},{96,128},{128,160},{160,192},{192,224},{224... | collective-permute-start | bytes 344072 | tf_op jit(solution)/shard_map/ppermute | solution.py:25
  239.1 21.3 %collective-permute-start.62 = (bf16[448,128]{1,0:T(8,128)(2,1)S(1)}, bf16[448,128]{1,0:T(8,128)(2,1)S(1)}, u32[]{:S(2)}, u32[]{:S(2)}) collective-permute-start(bf16[448,128]{1,0:T(8,128)(2,1)S(1)} %collective-permute-done.61.refs_20_), channel_id=1, source_target_pairs={{0,480},{32,0},{64,32},{96,64},{128,96},{160,128},{192,160},{224,1... | collective-permute-start | bytes 344072 | tf_op jit(solution)/shard_map/ppermute | solution.py:25
  244.9 18.1 %collective-permute-start.30 = (bf16[448,128]{1,0:T(8,128)(2,1)S(1)}, bf16[448,128]{1,0:T(8,128)(2,1)S(1)}, u32[]{:S(2)}, u32[]{:S(2)}) collective-permute-start(bf16[448,128]{1,0:T(8,128)(2,1)S(1)} %collective-permute-done.29.refs_2_), channel_id=1, source_target_pairs={{0,480},{32,0},{64,32},{96,64},{128,96},{160,128},{192,160},{224,1... | collective-permute-start | bytes 344072 | tf_op jit(solution)/shard_map/ppermute | solution.py:25
  249.5 19.3 %collective-permute-start.38 = (bf16[448,128]{1,0:T(8,128)(2,1)S(1)}, bf16[448,128]{1,0:T(8,128)(2,1)S(1)}, u32[]{:S(2)}, u32[]{:S(2)}) collective-permute-start(bf16[448,128]{1,0:T(8,128)(2,1)S(1)} %collective-permute-done.37.refs_13_), channel_id=1, source_target_pairs={{0,32},{32,64},{64,96},{96,128},{128,160},{160,192},{192,224},{224... | collective-permute-start | bytes 344072 | tf_op jit(solution)/shard_map/ppermute | solution.py:25
  252.0 19.3 %collective-permute-start.47 = (bf16[448,128]{1,0:T(8,128)(2,1)S(1)}, bf16[448,128]{1,0:T(8,128)(2,1)S(1)}, u32[]{:S(2)}, u32[]{:S(2)}) collective-permute-start(bf16[448,128]{1,0:T(8,128)(2,1)S(1)} %collective-permute-done.46.refs_4_), channel_id=1, source_target_pairs={{0,480},{32,0},{64,32},{96,64},{128,96},{160,128},{192,160},{224,1... | collective-permute-start | bytes 344072 | tf_op jit(solution)/shard_map/ppermute | solution.py:25
  257.8 19.3 %collective-permute-start.70 = (bf16[448,128]{1,0:T(8,128)(2,1)S(1)}, bf16[448,128]{1,0:T(8,128)(2,1)S(1)}, u32[]{:S(2)}, u32[]{:S(2)}) collective-permute-start(bf16[448,128]{1,0:T(8,128)(2,1)S(1)} %collective-permute-done.69.refs_28_), channel_id=1, source_target_pairs={{0,32},{32,64},{64,96},{96,128},{128,160},{160,192},{192,224},{224... | collective-permute-start | bytes 344072 | tf_op jit(solution)/shard_map/ppermute | solution.py:25
  260.4 20.1 %collective-permute-start.55 = (bf16[448,128]{1,0:T(8,128)(2,1)S(1)}, bf16[448,128]{1,0:T(8,128)(2,1)S(1)}, u32[]{:S(2)}, u32[]{:S(2)}) collective-permute-start(bf16[448,128]{1,0:T(8,128)(2,1)S(1)} %collective-permute-done.54.refs_11_), channel_id=1, source_target_pairs={{0,32},{32,64},{64,96},{96,128},{128,160},{160,192},{192,224},{224... | collective-permute-start | bytes 344072 | tf_op jit(solution)/shard_map/ppermute | solution.py:25
  263.0 21.3 %collective-permute-start.31 = (bf16[448,128]{1,0:T(8,128)(2,1)S(1)}, bf16[448,128]{1,0:T(8,128)(2,1)S(1)}, u32[]{:S(2)}, u32[]{:S(2)}) collective-permute-start(bf16[448,128]{1,0:T(8,128)(2,1)S(1)} %collective-permute-done.30.refs_3_), channel_id=1, source_target_pairs={{0,480},{32,0},{64,32},{96,64},{128,96},{160,128},{192,160},{224,1... | collective-permute-start | bytes 344072 | tf_op jit(solution)/shard_map/ppermute | solution.py:25
  268.7 20.1 %collective-permute-start.39 = (bf16[448,128]{1,0:T(8,128)(2,1)S(1)}, bf16[448,128]{1,0:T(8,128)(2,1)S(1)}, u32[]{:S(2)}, u32[]{:S(2)}) collective-permute-start(bf16[448,128]{1,0:T(8,128)(2,1)S(1)} %collective-permute-done.38.refs_12_), channel_id=1, source_target_pairs={{0,32},{32,64},{64,96},{96,128},{128,160},{160,192},{192,224},{224... | collective-permute-start | bytes 344072 | tf_op jit(solution)/shard_map/ppermute | solution.py:25
  271.3 20.1 %collective-permute-start.63 = (bf16[448,128]{1,0:T(8,128)(2,1)S(1)}, bf16[448,128]{1,0:T(8,128)(2,1)S(1)}, u32[]{:S(2)}, u32[]{:S(2)}) collective-permute-start(bf16[448,128]{1,0:T(8,128)(2,1)S(1)} %collective-permute-done.62.refs_21_), channel_id=1, source_target_pairs={{0,480},{32,0},{64,32},{96,64},{128,96},{160,128},{192,160},{224,1... | collective-permute-start | bytes 344072 | tf_op jit(solution)/shard_map/ppermute | solution.py:25
  277.1 16.9 %collective-permute-start.48 = (bf16[448,128]{1,0:T(8,128)(2,1)S(1)}, bf16[448,128]{1,0:T(8,128)(2,1)S(1)}, u32[]{:S(2)}, u32[]{:S(2)}) collective-permute-start(bf16[448,128]{1,0:T(8,128)(2,1)S(1)} %collective-permute-done.47.refs_5_), channel_id=1, source_target_pairs={{0,480},{32,0},{64,32},{96,64},{128,96},{160,128},{192,160},{224,1... | collective-permute-start | bytes 344072 | tf_op jit(solution)/shard_map/ppermute | solution.py:25
  280.4 19.3 %collective-permute-start.71 = (bf16[448,128]{1,0:T(8,128)(2,1)S(1)}, bf16[448,128]{1,0:T(8,128)(2,1)S(1)}, u32[]{:S(2)}, u32[]{:S(2)}) collective-permute-start(bf16[448,128]{1,0:T(8,128)(2,1)S(1)} %collective-permute-done.70.refs_27_), channel_id=1, source_target_pairs={{0,32},{32,64},{64,96},{96,128},{128,160},{160,192},{192,224},{224... | collective-permute-start | bytes 344072 | tf_op jit(solution)/shard_map/ppermute | solution.py:25
  284.2 20.0 %collective-permute-start.32 = (bf16[448,128]{1,0:T(8,128)(2,1)S(1)}, bf16[448,128]{1,0:T(8,128)(2,1)S(1)}, u32[]{:S(2)}, u32[]{:S(2)}) collective-permute-start(bf16[448,128]{1,0:T(8,128)(2,1)S(1)} %collective-permute-done.31.refs_4_), channel_id=1, source_target_pairs={{0,480},{32,0},{64,32},{96,64},{128,96},{160,128},{192,160},{224,1... | collective-permute-start | bytes 344072 | tf_op jit(solution)/shard_map/ppermute | solution.py:25
  288.8 18.2 %collective-permute-start.40 = (bf16[448,128]{1,0:T(8,128)(2,1)S(1)}, bf16[448,128]{1,0:T(8,128)(2,1)S(1)}, u32[]{:S(2)}, u32[]{:S(2)}) collective-permute-start(bf16[448,128]{1,0:T(8,128)(2,1)S(1)} %collective-permute-done.39.refs_11_), channel_id=1, source_target_pairs={{0,32},{32,64},{64,96},{96,128},{128,160},{160,192},{192,224},{224... | collective-permute-start | bytes 344072 | tf_op jit(solution)/shard_map/ppermute | solution.py:25
  291.4 20.0 %collective-permute-start.56 = (bf16[448,128]{1,0:T(8,128)(2,1)S(1)}, bf16[448,128]{1,0:T(8,128)(2,1)S(1)}, u32[]{:S(2)}, u32[]{:S(2)}) collective-permute-start(bf16[448,128]{1,0:T(8,128)(2,1)S(1)} %collective-permute-done.55.refs_10_), channel_id=1, source_target_pairs={{0,32},{32,64},{64,96},{96,128},{128,160},{160,192},{192,224},{224... | collective-permute-start | bytes 344072 | tf_op jit(solution)/shard_map/ppermute | solution.py:25
  293.9 20.0 %collective-permute-start.64 = (bf16[448,128]{1,0:T(8,128)(2,1)S(1)}, bf16[448,128]{1,0:T(8,128)(2,1)S(1)}, u32[]{:S(2)}, u32[]{:S(2)}) collective-permute-start(bf16[448,128]{1,0:T(8,128)(2,1)S(1)} %collective-permute-done.63.refs_22_), channel_id=1, source_target_pairs={{0,480},{32,0},{64,32},{96,64},{128,96},{160,128},{192,160},{224,1... | collective-permute-start | bytes 344072 | tf_op jit(solution)/shard_map/ppermute | solution.py:25
  299.7 16.8 %collective-permute-start.49 = (bf16[448,128]{1,0:T(8,128)(2,1)S(1)}, bf16[448,128]{1,0:T(8,128)(2,1)S(1)}, u32[]{:S(2)}, u32[]{:S(2)}) collective-permute-start(bf16[448,128]{1,0:T(8,128)(2,1)S(1)} %collective-permute-done.48.refs_6_), channel_id=1, source_target_pairs={{0,480},{32,0},{64,32},{96,64},{128,96},{160,128},{192,160},{224,1... | collective-permute-start | bytes 344072 | tf_op jit(solution)/shard_map/ppermute | solution.py:25
  304.3 18.7 %collective-permute-start.33 = (bf16[448,128]{1,0:T(8,128)(2,1)S(1)}, bf16[448,128]{1,0:T(8,128)(2,1)}, u32[]{:S(2)}, u32[]{:S(2)}) collective-permute-start(bf16[448,128]{1,0:T(8,128)(2,1)S(1)} %collective-permute-done.32.refs_5_), channel_id=1, source_target_pairs={{0,480},{32,0},{64,32},{96,64},{128,96},{160,128},{192,160},{224,1... | collective-permute-start | bytes 344072 | tf_op jit(solution)/shard_map/ppermute | solution.py:25
  307.0 19.8 %collective-permute-start.41 = (bf16[448,128]{1,0:T(8,128)(2,1)S(1)}, bf16[448,128]{1,0:T(8,128)(2,1)}, u32[]{:S(2)}, u32[]{:S(2)}) collective-permute-start(bf16[448,128]{1,0:T(8,128)(2,1)S(1)} %collective-permute-done.40.refs_10_), channel_id=1, source_target_pairs={{0,32},{32,64},{64,96},{96,128},{128,160},{160,192},{192,224},{224... | collective-permute-start | bytes 344072 | tf_op jit(solution)/shard_map/ppermute | solution.py:25
  311.4 17.6 %collective-permute-start.72 = (bf16[448,128]{1,0:T(8,128)(2,1)S(1)}, bf16[448,128]{1,0:T(8,128)(2,1)S(1)}, u32[]{:S(2)}, u32[]{:S(2)}) collective-permute-start(bf16[448,128]{1,0:T(8,128)(2,1)S(1)} %collective-permute-done.71.refs_26_), channel_id=1, source_target_pairs={{0,32},{32,64},{64,96},{96,128},{128,160},{160,192},{192,224},{224... | collective-permute-start | bytes 344072 | tf_op jit(solution)/shard_map/ppermute | solution.py:25
  314.0 15.7 %collective-permute-start.57 = (bf16[448,128]{1,0:T(8,128)(2,1)S(1)}, bf16[448,128]{1,0:T(8,128)(2,1)S(1)}, u32[]{:S(2)}, u32[]{:S(2)}) collective-permute-start(bf16[448,128]{1,0:T(8,128)(2,1)S(1)} %collective-permute-done.56.refs_9_), channel_id=1, source_target_pairs={{0,32},{32,64},{64,96},{96,128},{128,160},{160,192},{192,224},{224... | collective-permute-start | bytes 344072 | tf_op jit(solution)/shard_map/ppermute | solution.py:25
  317.2 13.2 %collective-permute-start.65 = (bf16[448,128]{1,0:T(8,128)(2,1)S(1)}, bf16[448,128]{1,0:T(8,128)(2,1)S(1)}, u32[]{:S(2)}, u32[]{:S(2)}) collective-permute-start(bf16[448,128]{1,0:T(8,128)(2,1)S(1)} %collective-permute-done.64.refs_23_), channel_id=1, source_target_pairs={{0,480},{32,0},{64,32},{96,64},{128,96},{160,128},{192,160},{224,1... | collective-permute-start | bytes 344072 | tf_op jit(solution)/shard_map/ppermute | solution.py:25
  323.0 36.9 %collective-permute-start.34 = (bf16[448,128]{1,0:T(8,128)(2,1)}, bf16[448,128]{1,0:T(8,128)(2,1)S(1)}, u32[]{:S(2)}, u32[]{:S(2)}) collective-permute-start(bf16[448,128]{1,0:T(8,128)(2,1)} %collective-permute-done.33.refs_6_), channel_id=1, source_target_pairs={{0,480},{32,0},{64,32},{96,64},{128,96},{160,128},{192,160},{224,1... | collective-permute-start | bytes 344072 | tf_op jit(solution)/shard_map/ppermute | solution.py:25
  326.9 32.9 %collective-permute-start.42 = (bf16[448,128]{1,0:T(8,128)(2,1)}, bf16[448,128]{1,0:T(8,128)(2,1)S(1)}, u32[]{:S(2)}, u32[]{:S(2)}) collective-permute-start(bf16[448,128]{1,0:T(8,128)(2,1)} %collective-permute-done.41.refs_9_), channel_id=1, source_target_pairs={{0,32},{32,64},{64,96},{96,128},{128,160},{160,192},{192,224},{224... | collective-permute-start | bytes 344072 | tf_op jit(solution)/shard_map/ppermute | solution.py:25
  369.0 8.7 %collective-permute-start.75 = (bf16[256,512]{1,0:T(8,128)(2,1)S(1)}, bf16[256,512]{1,0:T(8,128)(2,1)S(1)}, u32[]{:S(2)}, u32[]{:S(2)}) collective-permute-start(bf16[256,512]{1,0:T(8,128)(2,1)S(1)} %get-tuple-element.65), channel_id=1, source_target_pairs={{0,1},{1,0},{2,3},{3,2},{4,5},{5,4},{6,7},{7,6},{8,9},{9,8},{10,11... | collective-permute-start | bytes 786440 | tf_op jit(solution)/shard_map/ppermute | solution.py:38
  370.9 8.8 %collective-permute-start.74 = (bf16[256,512]{1,0:T(8,128)(2,1)S(1)}, bf16[256,512]{1,0:T(8,128)(2,1)S(1)}, u32[]{:S(2)}, u32[]{:S(2)}) collective-permute-start(bf16[256,512]{1,0:T(8,128)(2,1)S(1)} %get-tuple-element.63), channel_id=1, source_target_pairs={{0,1},{1,0},{2,3},{3,2},{4,5},{5,4},{6,7},{7,6},{8,9},{9,8},{10,11... | collective-permute-start | bytes 786440 | tf_op jit(solution)/shard_map/ppermute | solution.py:38
  373.3 11.6 %collective-permute-start.78 = (bf16[256,512]{1,0:T(8,128)(2,1)S(1)}, bf16[256,512]{1,0:T(8,128)(2,1)S(1)}, u32[]{:S(2)}, u32[]{:S(2)}) collective-permute-start(bf16[256,512]{1,0:T(8,128)(2,1)S(1)} %get-tuple-element.67), channel_id=1, source_target_pairs={{0,1},{1,0},{2,3},{3,2},{4,5},{5,4},{6,7},{7,6},{8,9},{9,8},{10,11... | collective-permute-start | bytes 786440 | tf_op jit(solution)/shard_map/ppermute | solution.py:38
  375.3 102.9 %collective-permute-start.73 = (bf16[256,512]{1,0:T(8,128)(2,1)S(1)}, bf16[256,512]{1,0:T(8,128)(2,1)S(1)}, u32[]{:S(2)}, u32[]{:S(2)}) collective-permute-start(bf16[256,512]{1,0:T(8,128)(2,1)S(1)} %get-tuple-element.61), channel_id=1, source_target_pairs={{0,1},{1,0},{2,3},{3,2},{4,5},{5,4},{6,7},{7,6},{8,9},{9,8},{10,11... | collective-permute-start | bytes 786440 | tf_op jit(solution)/shard_map/ppermute | solution.py:38
  386.4 91.8 %collective-permute-start.77 = (bf16[256,512]{1,0:T(8,128)(2,1)S(1)}, bf16[256,512]{1,0:T(8,128)(2,1)S(1)}, u32[]{:S(2)}, u32[]{:S(2)}) collective-permute-start(bf16[256,512]{1,0:T(8,128)(2,1)S(1)} %pad_maximum_fusion), channel_id=1, source_target_pairs={{0,8},{1,9},{2,10},{3,11},{4,12},{5,13},{6,14},{7,15},{8,16},{9,17... | collective-permute-start | bytes 786440 | tf_op jit(solution)/shard_map/ppermute | solution.py:38
  388.4 89.8 %collective-permute-start.80 = (bf16[256,512]{1,0:T(8,128)(2,1)S(1)}, bf16[256,512]{1,0:T(8,128)(2,1)S(1)}, u32[]{:S(2)}, u32[]{:S(2)}) collective-permute-start(bf16[256,512]{1,0:T(8,128)(2,1)S(1)} %pad_maximum_fusion.1), channel_id=1, source_target_pairs={{0,24},{1,25},{2,26},{3,27},{4,28},{5,29},{6,30},{7,31},{8,0},{9,1... | collective-permute-start | bytes 786440 | tf_op jit(solution)/shard_map/ppermute | solution.py:38
  478.3 20.9 %collective-permute-start.81 = (bf16[32,512]{1,0:T(8,128)(2,1)S(1)}, bf16[32,512]{1,0:T(8,128)(2,1)S(1)}, u32[]{:S(2)}, u32[]{:S(2)}) collective-permute-start(bf16[32,512]{1,0:T(8,128)(2,1)S(1)} %get-tuple-element.77), channel_id=1, source_target_pairs={{0,2},{1,3},{2,4},{3,5},{4,6},{5,7},{6,0},{7,1},{8,10},{9,11},{10,... | collective-permute-start | bytes 98312 | tf_op jit(solution)/shard_map/ppermute | solution.py:38
  (103 other events, 1155.4 us)
Sparse Core Ops, SparseCore 0:
  323.1 55.3 all-gather.3
